TPU v7x, 512 devices: a whole 4x8x8 slice. The times are simulated.
512 devices in a mesh: band: 8 (over y_lo, core), dom: 64 (over x, y_hi, z).
Axes of the slice: x: 4, y: 8 (y_hi: 2, y_lo: 4; y = y_hi * 4 + y_lo), z: 8, core: 2. Of those that a mesh axis runs over, the one named last changes fastest.
Arguments:
- states_in: float32 [512, 65536], P('band', 'dom'), may hold values from -6 to 6
- stiffness: float32 [343, 343], replicated, may hold values from -2 to 2, as said below
- cell_scale: float32 [384], P('dom'), may hold values from 0.5 to 2
- potential: float32 [65536], P('dom'), may hold values from 0 to 2
- inv_mass_sqrt: float32 [65536], P('dom'), may hold values from 0.25 to 1.75
- cell_nodes: int32 [384, 343], P('dom'), may hold values from 0 to 1151, as said below
- shared_nodes: int32 [8192], P('dom'), may hold values from 0 to 1023, as said below
Outputs:
- filtered: float32 [512, 65536], P('band', 'dom')
- margin: float32 [512, 512], P('band')
Inputs may be any that keep to these rules, and one draw needn't show every extreme that they name: `stiffness`: symmetric. `cell_nodes`: in the cells of a subdomain, an entry below 1024 is one of its own nodes and an entry l of 1024 or more stands for entry l - 1024 of the next subdomain's (cyclically) shared_nodes list; every value from 0 to 1151 occurs in the subdomain's cells. `shared_nodes`: the 128 entries of each subdomain are distinct.
All inputs are finite; a program needn't handle non-finite values.
Results may differ from a plain program's by a relative error of at most 0.0001.
Values sent between devices are 32-bit elements; how exact they have to be, the bound alone decides.
No kernel may reach another device: no remote copies, remote signals or barrier semaphores. Data moves between devices by JAX's collectives and lax.ppermute only.
A program may use at most 64 MiB of HBM per device.

v0:
```python
import jax
import jax.numpy as jnp
from jax import lax
from jax.sharding import PartitionSpec as P

DEGREE = 3
center_shift = 1.0
half_width = 4.0


def passed_along(x, axis, by):
    peers = lax.axis_size(axis)
    return lax.ppermute(x, axis, [(i, (i + by) % peers) for i in range(peers)])


def per_device(
    states_in, stiffness, cell_scale, potential, inv_mass_sqrt, cell_nodes, shared_nodes
):
    owned = states_in.shape[1]
    shared_count = shared_nodes.shape[0]
    block_rows = states_in.shape[0]

    def operate(vector):
        scaled = vector * inv_mass_sqrt[None, :]
        outgoing = jnp.take(scaled, shared_nodes, axis=1)
        ghosts = passed_along(outgoing, "dom", -1)
        extended = jnp.concatenate([scaled, ghosts], axis=1)
        cellwise = jnp.take(extended, cell_nodes, axis=1)
        product = jnp.einsum(
            "bcj,kj->bck",
            cellwise,
            stiffness,
            precision=lax.Precision.HIGHEST,
            preferred_element_type=jnp.float32,
        )
        product = product * cell_scale[None, :, None]
        summed = (
            jnp.zeros((block_rows, owned + shared_count), jnp.float32)
            .at[:, cell_nodes]
            .add(product)
        )
        returned = passed_along(summed[:, owned:], "dom", 1)
        own_sums = summed[:, :owned].at[:, shared_nodes].add(returned)
        return inv_mass_sqrt[None, :] * own_sums + potential[None, :] * vector

    previous = states_in
    current = (operate(states_in) - center_shift * states_in) / half_width
    for degree_step in range(DEGREE - 1):
        following = 2.0 * (operate(current) - center_shift * current) / half_width - previous
        previous = current
        current = following
    total_nodes = owned * lax.axis_size("dom")
    contract = (((1,), (1,)), ((), ()))
    pieces = lax.all_to_all(current, "band", split_axis=1, concat_axis=0, tiled=True)
    gram_local = lax.dot_general(
        pieces,
        pieces,
        contract,
        precision=lax.Precision.HIGHEST,
        preferred_element_type=jnp.float32,
    )
    summed_gram = lax.psum(gram_local, ("band", "dom"))
    row_block = lax.dynamic_slice_in_dim(
        summed_gram, lax.axis_index("band") * block_rows, block_rows, 0
    )
    return (current, row_block / total_nodes)


def solution(mesh):
    return jax.shard_map(
        per_device,
        mesh=mesh,
        in_specs=(P("band", "dom"), P(), P("dom"), P("dom"), P("dom"), P("dom", None), P("dom")),
        out_specs=(P("band", "dom"), P("band", None)),
        check_vma=False,
    )
```

profile of v0, /device:TPU:24, one launch (start us, length us, event | category | flops | bytes accessed | tf_op | source)
XLA Modules:
  0.0 459.4 jit_solution(5606167754359788286)
XLA Ops:
  7.2 0.0 copy-start
  7.2 0.0 all-reduce.2.cloned.1.call-start
  7.2 0.7 compare_select_fusion.1
  7.9 0.7 compare_and_fusion.1
  8.6 1.1 copy.17
  9.8 0.9 broadcast_multiply_fusion.2
  10.7 0.6 gather_fusion
  11.3 0.1 select_bitcast_fusion.5
  11.4 15.7 %collective-permute-start = (f32[64,128]{0,1:T(8,128)S(1)}, f32[64,128]{0,1:T(8,128)S(1)}, u32[]{:S(2)}, u32[]{:S(2)}) collective-permute-start(f32[64,128]{0,1:T(8,128)S(1)} %select_bitcast_fusion.5), channel_id=1, source_target_pairs={{0,63},{1,0},{2,1},{3,2},{4,3},{5,4},{6,5},{7,6},{8,7},{9,8},{10,9... | collective-permute-start | bytes 98312 | tf_op jit(solution)/shard_map/ppermute | solution.py:13
  27.2 0.1 reshape.102
  27.2 1.8 collective-permute-done
  29.0 3.9 gather_fusion.1
  33.0 0.3 copy.18
  33.3 0.4 reshape.139
  33.7 0.1 select_bitcast_fusion.2
  33.8 0.6 copy-done.4
  34.4 1.3 fusion
  35.7 0.3 copy.35
  36.0 0.1 reshape.153
  36.1 14.4 %scatter_custom_fusion = f32[64,1152]{0,1:T(8,128)S(1)} fusion(s32[2058]{0:T(1024)S(1)} %reshape.102, f32[2058,64]{1,0:T(8,128)S(1)} %reshape.153, f32[]{:T(128)} %constant.27.clone.1), kind=kCustom, calls=%fused_computation.37 | custom fusion | flops 131712 | bytes 294916 | tf_op jit(solution)/shard_map/scatter-add | solution.py:40
  50.5 1.9 collective-permute-start.1
  52.5 12.7 %collective-permute-done.1 = f32[64,128]{0,1:T(8,128)S(1)} collective-permute-done((f32[64,128]{0,1:T(8,128)S(1)}, f32[64,128]{0,1:T(8,128)S(1)}, u32[]{:S(2)}, u32[]{:S(2)}) %collective-permute-start.1) | collective-permute-done | bytes 32800 | tf_op jit(solution)/shard_map/ppermute | solution.py:13
  65.3 1.5 scatter_custom_fusion.1
  66.7 0.5 broadcast_multiply_fusion
  67.2 0.6 gather_fusion.2
  67.9 0.1 select_bitcast_fusion.4
  68.0 4.0 collective-permute-start.2
  72.0 2.1 collective-permute-done.2
  74.2 5.0 %gather_fusion.3 = f32[2058,64]{1,0:T(8,128)} fusion(f32[64,1152]{0,1:T(8,128)S(1)} %pad_maximum_fusion.1, s32[3072]{0:T(1024)S(1)} %pad_clamp_fusion), kind=kCustom, calls=%fused_computation.4.clone | custom fusion | bytes 1061928 | tf_op jit(solution)/shard_map/jit(_take)/gather | solution.py:28
  79.2 1.6 copy.24
  80.7 0.4 reshape.145
  81.1 0.1 select_bitcast_fusion.1
  81.2 1.3 fusion.1
  82.5 0.3 copy.36
  82.8 1.1 reshape.154
  83.9 14.7 %scatter_custom_fusion.2 = f32[64,1152]{0,1:T(8,128)S(1)} fusion(s32[2058]{0:T(1024)S(1)} %reshape.102, f32[2058,64]{1,0:T(8,128)} %reshape.154, f32[]{:T(128)} %constant.27.clone.1), kind=kCustom, calls=%fused_computation.35 | custom fusion | flops 131712 | bytes 295424 | tf_op jit(solution)/shard_map/scatter-add | solution.py:40
  98.7 1.9 collective-permute-start.3
  100.6 12.3 %collective-permute-done.3 = f32[64,128]{0,1:T(8,128)S(1)} collective-permute-done((f32[64,128]{0,1:T(8,128)S(1)}, f32[64,128]{0,1:T(8,128)S(1)}, u32[]{:S(2)}, u32[]{:S(2)}) %collective-permute-start.3) | collective-permute-done | bytes 32800 | tf_op jit(solution)/shard_map/ppermute | solution.py:13
  112.9 1.5 scatter_custom_fusion.3
  114.4 0.5 broadcast_multiply_fusion.1
  114.9 0.6 gather_fusion.4
  115.5 0.1 select_bitcast_fusion.3
  115.6 3.8 collective-permute-start.4
  119.5 2.3 collective-permute-done.4
  121.8 5.0 %gather_fusion.5 = f32[2058,64]{1,0:T(8,128)} fusion(f32[64,1152]{0,1:T(8,128)S(1)} %pad_maximum_fusion.2, s32[3072]{0:T(1024)S(1)} %pad_clamp_fusion), kind=kCustom, calls=%fused_computation.5.clone | custom fusion | bytes 1061928 | tf_op jit(solution)/shard_map/jit(_take)/gather | solution.py:28
  126.8 2.4 copy.29
  129.2 1.4 reshape.151
  130.6 0.1 select_bitcast_fusion
  130.7 1.3 fusion.2
  132.0 1.3 copy.37
  133.4 2.3 reshape.155
  135.7 14.7 %scatter_custom_fusion.4 = f32[64,1152]{0,1:T(8,128)S(1)} fusion(s32[2058]{0:T(1024)S(1)} %reshape.102, f32[2058,64]{1,0:T(8,128)} %reshape.155, f32[]{:T(128)} %constant.27.clone.1), kind=kCustom, calls=%fused_computation.33 | custom fusion | flops 131712 | bytes 295424 | tf_op jit(solution)/shard_map/scatter-add | solution.py:40
  150.4 1.9 collective-permute-start.5
  152.4 0.8 slice.40
  153.2 11.5 %collective-permute-done.5 = f32[64,128]{0,1:T(8,128)S(1)} collective-permute-done((f32[64,128]{0,1:T(8,128)S(1)}, f32[64,128]{0,1:T(8,128)S(1)}, u32[]{:S(2)}, u32[]{:S(2)}) %collective-permute-start.5) | collective-permute-done | bytes 32800 | tf_op jit(solution)/shard_map/ppermute | solution.py:13
  164.7 3.0 scatter_custom_fusion.5
  167.7 1.5 multiply_subtract_fusion
  169.2 0.2 copy.33
  169.4 14.5 %all_to_all.19 = f32[64,8,128]{2,0,1:T(8,128)S(1)} all-to-all(f32[64,8,128]{2,0,1:T(8,128)S(1)} %copy.33), channel_id=1, replica_groups=mesh['band'=8,'dom'=64] {'band'}, dimensions={1} | all-to-all | bytes 524288 | tf_op jit(solution)/shard_map/all_to_all | solution.py:54
  183.9 2.0 fusion.21
  185.9 0.0 all-reduce.2.cloned.1.call-update
  186.0 0.9 copy.34
  186.8 264.2 %all-reduce.2.cloned.1.call-done = f32[512,512]{1,0:T(8,128)} async-done(((f32[512,512]{1,0:T(8,128)}), f32[512,512]{1,0:T(8,128)}) %all-reduce.2.cloned.1.call-update) | async-done | bytes 1048592 | tf_op jit(solution)/shard_map/psum | solution.py:62
  451.0 1.6 dynamic-slice_multiply_fusion
  (22 shorter events, 0.3 us)
Async XLA Ops:
  7.2 26.6 %copy-start = (f32[343,343]{1,0:T(8,128)S(1)}, f32[343,343]{1,0:T(8,128)}, u32[]{:S(2)}) copy-start(f32[343,343]{1,0:T(8,128)} %param.12) | copy-start | bytes 1411792
  7.2 443.9 %all-reduce.2.cloned.1.call-start = ((), (), s32[]{:S(2)}) async-start(), calls=%async_computation.1 | async-start | bytes 2097152 | tf_op jit(solution)/shard_map/psum | solution.py:62
  8.6 18.5 %copy-start.3 = (s32[6,343]{1,0:T(8,128)S(1)}, s32[6,343]{1,0:T(8,128)}, u32[]{:S(2)}) copy-start(s32[6,343]{1,0:T(8,128)} %param.16) | copy-start | bytes 24700
  11.4 17.6 %collective-permute-start = (f32[64,128]{0,1:T(8,128)S(1)}, f32[64,128]{0,1:T(8,128)S(1)}, u32[]{:S(2)}, u32[]{:S(2)}) collective-permute-start(f32[64,128]{0,1:T(8,128)S(1)} %select_bitcast_fusion.5), channel_id=1, source_target_pairs={{0,63},{1,0},{2,1},{3,2},{4,3},{5,4},{6,5},{7,6},{8,7},{9,8},{10,9... | collective-permute-start | bytes 98312 | tf_op jit(solution)/shard_map/ppermute | solution.py:13
  33.7 0.7 copy-start.4
  36.0 16.4 %copy-start.1 = (f32[1024]{0:T(1024)S(1)}, f32[1024]{0:T(1024)}, u32[]{:S(2)}) copy-start(f32[1024]{0:T(1024)} %param.15) | copy-start | bytes 12292
  36.1 30.6 %copy-start.2 = (f32[1024]{0:T(1024)S(1)}, f32[1024]{0:T(1024)}, u32[]{:S(2)}) copy-start(f32[1024]{0:T(1024)} %param.14) | copy-start | bytes 12292
  50.5 14.7 %collective-permute-start.1 = (f32[64,128]{0,1:T(8,128)S(1)}, f32[64,128]{0,1:T(8,128)S(1)}, u32[]{:S(2)}, u32[]{:S(2)}) collective-permute-start(f32[64,128]{0,1:T(8,128)S(1)} %slice.37), channel_id=1, source_target_pairs={{0,1},{1,2},{2,3},{3,4},{4,5},{5,6},{6,7},{7,8},{8,9},{9,10},{10,1... | collective-permute-start | bytes 98312 | tf_op jit(solution)/shard_map/ppermute | solution.py:13
  68.0 6.2 %collective-permute-start.2 = (f32[64,128]{0,1:T(8,128)S(1)}, f32[64,128]{0,1:T(8,128)S(1)}, u32[]{:S(2)}, u32[]{:S(2)}) collective-permute-start(f32[64,128]{0,1:T(8,128)S(1)} %select_bitcast_fusion.4), channel_id=1, source_target_pairs={{0,63},{1,0},{2,1},{3,2},{4,3},{5,4},{6,5},{7,6},{8,7},{9,8},{10,9... | collective-permute-start | bytes 98312 | tf_op jit(solution)/shard_map/ppermute | solution.py:13
  98.7 14.3 %collective-permute-start.3 = (f32[64,128]{0,1:T(8,128)S(1)}, f32[64,128]{0,1:T(8,128)S(1)}, u32[]{:S(2)}, u32[]{:S(2)}) collective-permute-start(f32[64,128]{0,1:T(8,128)S(1)} %slice.39), channel_id=1, source_target_pairs={{0,1},{1,2},{2,3},{3,4},{4,5},{5,6},{6,7},{7,8},{8,9},{9,10},{10,1... | collective-permute-start | bytes 98312 | tf_op jit(solution)/shard_map/ppermute | solution.py:13
  115.6 6.2 %collective-permute-start.4 = (f32[64,128]{0,1:T(8,128)S(1)}, f32[64,128]{0,1:T(8,128)S(1)}, u32[]{:S(2)}, u32[]{:S(2)}) collective-permute-start(f32[64,128]{0,1:T(8,128)S(1)} %select_bitcast_fusion.3), channel_id=1, source_target_pairs={{0,63},{1,0},{2,1},{3,2},{4,3},{5,4},{6,5},{7,6},{8,7},{9,8},{10,9... | collective-permute-start | bytes 98312 | tf_op jit(solution)/shard_map/ppermute | solution.py:13
  150.4 14.3 %collective-permute-start.5 = (f32[64,128]{0,1:T(8,128)S(1)}, f32[64,128]{0,1:T(8,128)S(1)}, u32[]{:S(2)}, u32[]{:S(2)}) collective-permute-start(f32[64,128]{0,1:T(8,128)S(1)} %slice.41), channel_id=1, source_target_pairs={{0,1},{1,2},{2,3},{3,4},{4,5},{5,6},{6,7},{7,8},{8,9},{9,10},{10,1... | collective-permute-start | bytes 98312 | tf_op jit(solution)/shard_map/ppermute | solution.py:13
Sparse Core Ops, SparseCore 0:
  186.1 264.9 all-reduce.1
where the time goes:
time: 460 us; the launch traced here: 459 us
  waiting for transfers between devices  307 us (67%)
  other arithmetic  56.7 us (12%)
  local copies, waits for them, and re-layouts  31.6 us (7%)
  starting transfers between devices  29.3 us (6%)
  blocking collectives  14.5 us (3%)
  between operations  14.5 us (3%)
  matrix products  5.91 us (1%)
    psum x1, waiting for transfers between devices, per_device(): summed_gram = lax.psum(gram_local, ('band', 'dom'))  264 us
    scatter-add x3, other arithmetic, operate(): summed = jnp.zeros((block_rows, owned + shared_count), jnp.float32).at[:,...  43.8 us
    ppermute x6, waiting for transfers between devices, passed_along(): return lax.ppermute(x, axis, [(i, (i + by) % peers) for i in range(peers)])  42.8 us
    ppermute x6, starting transfers between devices, passed_along(): return lax.ppermute(x, axis, [(i, (i + by) % peers) for i in range(peers)])  29.3 us
    gather x9, local copies, waits for them, and re-layouts, operate(): cellwise = jnp.take(extended, cell_nodes, axis=1)  20.4 us
    all_to_all x1, blocking collectives, per_device(): lax.all_to_all(current, 'band', split_axis=1, concat_axis=0, tiled=True)  14.5 us
  transfers between devices with their start and end apart: 7, of which 7 were waited for; matrix products, arithmetic and copies ran while one was open for 0% of the time, Pallas kernels for 0%

commit v1 on v0

--- a/solution.py
+++ b/solution.py
@@ -59,7 +59,7 @@
         precision=lax.Precision.HIGHEST,
         preferred_element_type=jnp.float32,
     )
-    summed_gram = lax.psum(gram_local, ("band", "dom"))
+    summed_gram = lax.psum(lax.psum(gram_local, "dom"), "band")
     row_block = lax.dynamic_slice_in_dim(
         summed_gram, lax.axis_index("band") * block_rows, block_rows, 0
     )

time: 460 us -> 1110 us (2.41)
  the two profiles are of different devices: /device:TPU:24 before, /device:TPU:2 now
where the time goes in v1:
time: 1110 us
  waiting for transfers between devices  957 us (86%)
  other arithmetic  56.7 us (5%)
  local copies, waits for them, and re-layouts  31.6 us (3%)
  starting transfers between devices  30 us (3%)
  between operations  14.5 us (1%)
  blocking collectives  12.9 us (1%)
    psum x2, waiting for transfers between devices, per_device(): summed_gram = lax.psum(lax.psum(gram_local, 'dom'), 'band')  917 us
    scatter-add x3, other arithmetic, operate(): summed = jnp.zeros((block_rows, owned + shared_count), jnp.float32).at[:,...  43.8 us
    ppermute x6, waiting for transfers between devices, passed_along(): return lax.ppermute(x, axis, [(i, (i + by) % peers) for i in range(peers)])  39.8 us
    ppermute x6, starting transfers between devices, passed_along(): return lax.ppermute(x, axis, [(i, (i + by) % peers) for i in range(peers)])  30 us
  transfers between devices with their start and end apart: 8, of which 8 were waited for; matrix products, arithmetic and copies ran while one was open for 0% of the time, Pallas kernels for 0%

profile of v1, /device:TPU:2, one launch (start us, length us, event | category | flops | bytes accessed | tf_op | source)
XLA Modules:
  0.0 1108.1 jit_solution(12728195200413404552)
XLA Ops:
  7.2 0.0 all-reduce.3.cloned.1.call-start
  7.2 0.7 compare_select_fusion.1
  7.9 0.7 compare_and_fusion.1
  8.6 1.1 copy.17
  9.8 0.9 broadcast_multiply_fusion.2
  10.7 0.6 gather_fusion
  11.3 0.1 select_bitcast_fusion.5
  11.4 16.2 %collective-permute-start = (f32[64,128]{0,1:T(8,128)S(1)}, f32[64,128]{0,1:T(8,128)S(1)}, u32[]{:S(2)}, u32[]{:S(2)}) collective-permute-start(f32[64,128]{0,1:T(8,128)S(1)} %select_bitcast_fusion.5), channel_id=1, source_target_pairs={{0,63},{1,0},{2,1},{3,2},{4,3},{5,4},{6,5},{7,6},{8,7},{9,8},{10,9... | collective-permute-start | bytes 98312 | tf_op jit(solution)/shard_map/ppermute | solution.py:13
  27.6 0.1 reshape.102
  27.7 2.6 collective-permute-done
  30.4 3.9 gather_fusion.1
  34.3 0.3 copy.18
  34.7 0.4 reshape.139
  35.1 0.1 select_bitcast_fusion.2
  35.2 0.6 copy-done.4
  35.7 1.3 fusion
  37.0 0.3 copy.35
  37.4 0.1 reshape.153
  37.5 14.4 %scatter_custom_fusion = f32[64,1152]{0,1:T(8,128)S(1)} fusion(s32[2058]{0:T(1024)S(1)} %reshape.102, f32[2058,64]{1,0:T(8,128)S(1)} %reshape.153, f32[]{:T(128)} %constant.27.clone.1), kind=kCustom, calls=%fused_computation.37 | custom fusion | flops 131712 | bytes 294916 | tf_op jit(solution)/shard_map/scatter-add | solution.py:40
  51.9 1.9 collective-permute-start.1
  53.9 11.5 %collective-permute-done.1 = f32[64,128]{0,1:T(8,128)S(1)} collective-permute-done((f32[64,128]{0,1:T(8,128)S(1)}, f32[64,128]{0,1:T(8,128)S(1)}, u32[]{:S(2)}, u32[]{:S(2)}) %collective-permute-start.1) | collective-permute-done | bytes 32800 | tf_op jit(solution)/shard_map/ppermute | solution.py:13
  65.4 1.5 scatter_custom_fusion.1
  66.9 0.5 broadcast_multiply_fusion
  67.3 0.6 gather_fusion.2
  68.0 0.1 select_bitcast_fusion.4
  68.1 4.1 collective-permute-start.2
  72.2 2.0 collective-permute-done.2
  74.3 5.0 gather_fusion.3
  79.3 1.6 copy.24
  80.9 0.4 reshape.145
  81.2 0.1 select_bitcast_fusion.1
  81.3 1.3 fusion.1
  82.6 0.3 copy.36
  83.0 1.1 reshape.154
  84.0 14.7 %scatter_custom_fusion.2 = f32[64,1152]{0,1:T(8,128)S(1)} fusion(s32[2058]{0:T(1024)S(1)} %reshape.102, f32[2058,64]{1,0:T(8,128)} %reshape.154, f32[]{:T(128)} %constant.27.clone.1), kind=kCustom, calls=%fused_computation.35 | custom fusion | flops 131712 | bytes 295424 | tf_op jit(solution)/shard_map/scatter-add | solution.py:40
  98.8 1.9 collective-permute-start.3
  100.8 11.1 %collective-permute-done.3 = f32[64,128]{0,1:T(8,128)S(1)} collective-permute-done((f32[64,128]{0,1:T(8,128)S(1)}, f32[64,128]{0,1:T(8,128)S(1)}, u32[]{:S(2)}, u32[]{:S(2)}) %collective-permute-start.3) | collective-permute-done | bytes 32800 | tf_op jit(solution)/shard_map/ppermute | solution.py:13
  111.9 1.5 scatter_custom_fusion.3
  113.3 0.5 broadcast_multiply_fusion.1
  113.8 0.6 gather_fusion.4
  114.5 0.1 select_bitcast_fusion.3
  114.5 3.9 collective-permute-start.4
  118.5 2.2 collective-permute-done.4
  120.7 5.0 gather_fusion.5
  125.8 2.4 copy.29
  128.2 1.4 reshape.151
  129.6 0.1 select_bitcast_fusion
  129.7 1.3 fusion.2
  131.0 1.3 copy.37
  132.3 2.3 reshape.155
  134.6 14.7 %scatter_custom_fusion.4 = f32[64,1152]{0,1:T(8,128)S(1)} fusion(s32[2058]{0:T(1024)S(1)} %reshape.102, f32[2058,64]{1,0:T(8,128)} %reshape.155, f32[]{:T(128)} %constant.27.clone.1), kind=kCustom, calls=%fused_computation.33 | custom fusion | flops 131712 | bytes 295424 | tf_op jit(solution)/shard_map/scatter-add | solution.py:40
  149.4 1.9 collective-permute-start.5
  151.3 0.8 slice.40
  152.1 10.3 collective-permute-done.5
  162.4 3.0 scatter_custom_fusion.5
  165.4 1.5 multiply_subtract_fusion
  166.9 0.2 copy.33
  167.1 12.9 %all_to_all.19 = f32[64,8,128]{2,0,1:T(8,128)S(1)} all-to-all(f32[64,8,128]{2,0,1:T(8,128)S(1)} %copy.33), channel_id=1, replica_groups=mesh['band'=8,'dom'=64] {'band'}, dimensions={1} | all-to-all | bytes 524288 | tf_op jit(solution)/shard_map/all_to_all | solution.py:54
  180.0 2.0 fusion.21
  182.0 0.0 all-reduce.5.cloned.1.call-start
  182.1 803.4 %all-reduce.3.cloned.1.call-done = f32[512,512]{1,0:T(8,128)} async-done(((f32[512,512]{1,0:T(8,128)}), f32[512,512]{1,0:T(8,128)}) %all-reduce.3.cloned.1.call-update) | async-done | bytes 1048592 | tf_op jit(solution)/shard_map/psum | solution.py:62
  985.5 0.9 copy.34
  986.4 113.2 %all-reduce.5.cloned.1.call-done = f32[512,512]{1,0:T(8,128)} async-done(((f32[512,512]{1,0:T(8,128)}), f32[512,512]{1,0:T(8,128)}) %all-reduce.5.cloned.1.call-update) | async-done | bytes 1048592 | tf_op jit(solution)/shard_map/psum | solution.py:62
  1099.7 1.6 dynamic-slice_multiply_fusion
  (25 shorter events, 0.3 us)
Async XLA Ops:
  7.2 28.0 %copy-start = (f32[343,343]{1,0:T(8,128)S(1)}, f32[343,343]{1,0:T(8,128)}, u32[]{:S(2)}) copy-start(f32[343,343]{1,0:T(8,128)} %param.12) | copy-start | bytes 1411792
  7.2 978.3 %all-reduce.3.cloned.1.call-start = ((), (), s32[]{:S(2)}) async-start(), calls=%async_computation.1 | async-start | bytes 2097152 | tf_op jit(solution)/shard_map/psum | solution.py:62
  8.6 19.0 %copy-start.3 = (s32[6,343]{1,0:T(8,128)S(1)}, s32[6,343]{1,0:T(8,128)}, u32[]{:S(2)}) copy-start(s32[6,343]{1,0:T(8,128)} %param.16) | copy-start | bytes 24700
  11.4 19.0 %collective-permute-start = (f32[64,128]{0,1:T(8,128)S(1)}, f32[64,128]{0,1:T(8,128)S(1)}, u32[]{:S(2)}, u32[]{:S(2)}) collective-permute-start(f32[64,128]{0,1:T(8,128)S(1)} %select_bitcast_fusion.5), channel_id=1, source_target_pairs={{0,63},{1,0},{2,1},{3,2},{4,3},{5,4},{6,5},{7,6},{8,7},{9,8},{10,9... | collective-permute-start | bytes 98312 | tf_op jit(solution)/shard_map/ppermute | solution.py:13
  35.1 0.7 copy-start.4
  37.4 16.4 %copy-start.1 = (f32[1024]{0:T(1024)S(1)}, f32[1024]{0:T(1024)}, u32[]{:S(2)}) copy-start(f32[1024]{0:T(1024)} %param.15) | copy-start | bytes 12292
  37.5 29.4 %copy-start.2 = (f32[1024]{0:T(1024)S(1)}, f32[1024]{0:T(1024)}, u32[]{:S(2)}) copy-start(f32[1024]{0:T(1024)} %param.14) | copy-start | bytes 12292
  51.9 13.5 %collective-permute-start.1 = (f32[64,128]{0,1:T(8,128)S(1)}, f32[64,128]{0,1:T(8,128)S(1)}, u32[]{:S(2)}, u32[]{:S(2)}) collective-permute-start(f32[64,128]{0,1:T(8,128)S(1)} %slice.37), channel_id=1, source_target_pairs={{0,1},{1,2},{2,3},{3,4},{4,5},{5,6},{6,7},{7,8},{8,9},{9,10},{10,1... | collective-permute-start | bytes 98312 | tf_op jit(solution)/shard_map/ppermute | solution.py:13
  68.1 6.2 collective-permute-start.2
  98.8 13.1 %collective-permute-start.3 = (f32[64,128]{0,1:T(8,128)S(1)}, f32[64,128]{0,1:T(8,128)S(1)}, u32[]{:S(2)}, u32[]{:S(2)}) collective-permute-start(f32[64,128]{0,1:T(8,128)S(1)} %slice.39), channel_id=1, source_target_pairs={{0,1},{1,2},{2,3},{3,4},{4,5},{5,6},{6,7},{7,8},{8,9},{9,10},{10,1... | collective-permute-start | bytes 98312 | tf_op jit(solution)/shard_map/ppermute | solution.py:13
  114.5 6.2 collective-permute-start.4
  149.4 13.1 %collective-permute-start.5 = (f32[64,128]{0,1:T(8,128)S(1)}, f32[64,128]{0,1:T(8,128)S(1)}, u32[]{:S(2)}, u32[]{:S(2)}) collective-permute-start(f32[64,128]{0,1:T(8,128)S(1)} %slice.41), channel_id=1, source_target_pairs={{0,1},{1,2},{2,3},{3,4},{4,5},{5,6},{6,7},{7,8},{8,9},{9,10},{10,1... | collective-permute-start | bytes 98312 | tf_op jit(solution)/shard_map/ppermute | solution.py:13
  182.0 917.6 %all-reduce.5.cloned.1.call-start = ((), (), s32[]{:S(2)}) async-start(), calls=%async_computation.2 | async-start | bytes 2097152 | tf_op jit(solution)/shard_map/psum | solution.py:62
Sparse Core Ops, SparseCore 0:
  182.2 803.3 all-reduce.2
  988.7 110.9 all-reduce.4
